TPU v7x, 512 devices: a whole 4x4x16 slice. The times are simulated.
512 devices in a mesh: tm: 32 (over x_hi, z), head: 16 (over x_lo, y, core).
Axes of the slice: x: 4 (x_hi: 2, x_lo: 2; x = x_hi * 2 + x_lo), y: 4, z: 16, core: 2. Of those that a mesh axis runs over, the one named last changes fastest.
Arguments:
- queries: bfloat16 [73728, 4096], P(('tm', 'head')), may hold values from -8 to 8
- keys: bfloat16 [73728, 4096], P(('tm', 'head')), may hold values from -8 to 8
- values: bfloat16 [73728, 4096], P(('tm', 'head')), may hold values from -6 to 6
- tile_list: int32 [192, 7], P('tm'), may hold values from 0 to 191, as said below
- tile_count: int32 [192], P('tm'), may hold values from 1 to 7
Outputs:
- attended: bfloat16 [73728, 4096], P(('tm', 'head'))
Inputs may be any that keep to these rules, and one draw needn't show every extreme that they name: `tile_list`: row t lists distinct tiles of t's time slab (tiles t // 6 * 6 and on) and of the slabs just before and after it; the first slot is t itself; every slot holds such a tile, also past the count.
All inputs are finite; a program needn't handle non-finite values.
Results may differ from a plain program's by a relative error of at most 0.0046.
Values may be sent and summed in bfloat16 or wider, within the bound.
A program may use at most 64 MiB of HBM per device.

v0:
```python
import jax
import jax.numpy as jnp
from jax import lax
from jax.sharding import Mesh
from jax.sharding import PartitionSpec as P

HD = 128
TILE = 384
HEAD = ("head_0", "head_1", "head_2")
TM_HEAD = ("tm", "head_0", "head_1", "head_2")


def with_halo(block, sides, width):
    for axis, dim in sides:
        count = lax.axis_size(axis)
        forward = [(i, i + 1) for i in range(count - 1)]
        backward = [(target, source) for source, target in forward]
        low = lax.ppermute(
            lax.slice_in_dim(block, block.shape[dim] - width, None, axis=dim), axis, forward
        )
        high = lax.ppermute(lax.slice_in_dim(block, 0, width, axis=dim), axis, backward)
        block = jnp.concatenate([low, block, high], axis=dim)
    return block


def cut_along(x, dim, length):
    shape = x.shape
    blocks = x.reshape(*shape[:dim], length, shape[dim] // length, *shape[dim + 1 :])
    return jnp.moveaxis(blocks, dim, 0)


def in_order(blocks, dim):
    blocks = jnp.moveaxis(blocks, 0, dim)
    shape = blocks.shape
    return blocks.reshape(*shape[:dim], shape[dim] * shape[dim + 1], *shape[dim + 2 :])


def moved_by_axis(blocks, axes, order):
    shape = [lax.axis_size(a) for a in axes]
    blocks = blocks.reshape(*shape, *blocks.shape[1:])
    for k in order:
        blocks = lax.all_to_all(blocks, axes[k], split_axis=k, concat_axis=k, tiled=True)
    return blocks.reshape(-1, *blocks.shape[len(axes) :])


def two_step_exchange(x, groups, order, split_dim, concat_dim):
    length = lax.axis_size(groups[0]) * lax.axis_size(groups[1])
    blocks = cut_along(x, split_dim, length)
    return in_order(moved_by_axis(blocks, groups, order), concat_dim)


def attend(queries, key_ext, value_ext, tile_list, tile_count, offset_base):
    tiles = tile_list.shape[0]
    head_count = queries.shape[1]
    key_tiles = key_ext.reshape(3 * tiles, TILE, head_count, HD)
    value_tiles = value_ext.reshape(3 * tiles, TILE, head_count, HD)
    local_list = tile_list - offset_base
    key_span = tile_list.shape[1] * TILE
    slot_tile = jnp.arange(key_span, dtype=jnp.int32) // TILE
    scaling = HD ** (-0.5)

    def per_tile(operands):
        query_tile, listed, live_count = operands
        key_block = jnp.take(key_tiles, listed, axis=0).reshape(key_span, head_count, HD)
        value_block = jnp.take(value_tiles, listed, axis=0).reshape(key_span, head_count, HD)
        scores = (
            jnp.einsum("qhd,khd->hqk", query_tile, key_block, preferred_element_type=jnp.float32)
            * scaling
        )
        live_slots = slot_tile < live_count
        scores = jnp.where(live_slots[None, None, :], scores, -jnp.inf)
        highest = jnp.max(scores, axis=-1, keepdims=True)
        raised = jnp.exp(scores - highest)
        totals = jnp.sum(raised, axis=-1)
        weights = raised.astype(jnp.bfloat16)
        accumulated = jnp.einsum(
            "hqk,khd->qhd", weights, value_block, preferred_element_type=jnp.float32
        )
        return (accumulated / jnp.transpose(totals)[:, :, None]).astype(jnp.bfloat16)

    output = lax.map(
        per_tile, (queries.reshape(tiles, TILE, head_count, HD), local_list, tile_count)
    )
    return output.reshape(tiles * TILE, head_count, HD)


def shards(queries, keys, values, tile_list, tile_count):
    groups = lax.axis_size(HEAD)
    tok_dev, row_width = queries.shape
    head_dev = row_width // (groups * HD)
    query_six = queries.reshape(1, tok_dev, 1, groups, head_dev, HD)
    paired = jnp.stack([keys, values], axis=1).reshape(1, tok_dev, 2, groups, head_dev, HD)
    offset_base = (lax.axis_index("tm") - 1) * tile_list.shape[0]
    query_piece = lax.all_to_all(query_six, HEAD, split_axis=3, concat_axis=1, tiled=True)
    pair_piece = lax.all_to_all(paired, HEAD, split_axis=3, concat_axis=1, tiled=True)
    slab_rows = query_piece.shape[1]
    head_count = query_piece.shape[4]
    extended = with_halo(pair_piece, (("tm", 1),), slab_rows)
    extended = extended.reshape(3 * slab_rows, 2, head_count, HD)
    output = attend(
        query_piece.reshape(slab_rows, head_count, HD),
        extended[:, 0],
        extended[:, 1],
        tile_list,
        tile_count,
        offset_base,
    )
    result = output.reshape(slab_rows, 1, head_count, HD)
    slab_rows = result.shape[0]
    restored = two_step_exchange(
        result.reshape(slab_rows, 1, head_dev * HD), (("head_0", "head_1"), "head_2"), (1, 0), 0, 1
    )
    return restored.reshape(tok_dev, row_width)


def solution(mesh):
    torus = Mesh(
        mesh.devices.reshape(mesh.shape["tm"], 2, 4, 2), ("tm", "head_0", "head_1", "head_2")
    )
    in_specs = (P(TM_HEAD, None), P(TM_HEAD, None), P(TM_HEAD, None), P("tm", None), P("tm"))
    out_specs = P(TM_HEAD, None)
    return jax.shard_map(
        shards, mesh=torus, in_specs=in_specs, out_specs=out_specs, check_vma=False
    )
```

profile of v0, /device:TPU:1, one launch (start us, length us, event | category | flops | bytes accessed | tf_op | source)
XLA Modules:
  0.0 301.5 jit_solution(13790420991502447111)
XLA Ops:
  0.0 3.4 %stack.10 = bf16[1,144,1,16,2,128]{5,4,3,1,2,0:T(2,128)(2,1)S(1)} reshape(bf16[144,4096]{1,0:T(8,128)(2,1)} %param.11) | data formatting | bytes 2359296 | tf_op jit(solution)/shard_map/stack | solution.py:92
  4.3 3.3 %pad_maximum_fusion = bf16[1,144,2,16,2,128]{5,4,3,1,2,0:T(2,128)(2,1)S(1)} fusion(bf16[1,144,1,16,2,128]{5,4,3,1,2,0:T(2,128)(2,1)S(1)} %stack.10, bf16[1,144,1,16,2,128]{5,4,3,1,2,0:T(2,128)(2,1)S(1)} %stack.9), kind=kLoop, calls=%fused_computation.39 | loop fusion | flops 1179648 | bytes 4718592 | tf_op jit(solution)/shard_map/stack | solution.py:92
  9.8 39.0 %all_to_all.43 = bf16[1,144,2,16,2,128]{5,4,1,2,0,3:T(2,128)(2,1)S(1)} all-to-all(bf16[1,144,2,16,2,128]{5,4,1,2,0,3:T(2,128)(2,1)S(1)} %copy.33), channel_id=1, replica_groups=mesh['tm'=32,'head_0'=2,'head_1'=4,'head_2'=2] {'head_0','head_1','head_2'}, dimensions={3} | all-to-all | bytes 4718592 | tf_op jit(solution)/shard_map/all_to_all | solution.py:95
  49.1 2.7 collective-permute-start
  53.1 3.3 %reshape.32 = bf16[1,144,1,16,2,128]{5,4,3,1,2,0:T(2,128)(2,1)S(1)} reshape(bf16[144,4096]{1,0:T(8,128)(2,1)} %param.9) | data formatting | bytes 2359296 | tf_op jit(solution)/shard_map/reshape | solution.py:91
  58.4 4.5 %all-to-all-start.1 = ((bf16[1,144,1,16,2,128]{5,4,1,2,0,3:T(2,128)(2,1)}), bf16[1,144,1,16,2,128]{5,4,1,2,0,3:T(2,128)(2,1)S(1)}, u32[]{:S(2)}, u32[]{:S(2)}) async-start(bf16[1,144,1,16,2,128]{5,4,1,2,0,3:T(2,128)(2,1)} %copy.35), calls=%async_computation.1 | async-start | bytes 2359296 | tf_op jit(solution)/shard_map/all_to_all | solution.py:94
  62.9 60.3 %all-to-all-done.1 = bf16[1,144,1,16,2,128]{5,4,1,2,0,3:T(2,128)(2,1)S(1)} async-done(((bf16[1,144,1,16,2,128]{5,4,1,2,0,3:T(2,128)(2,1)}), bf16[1,144,1,16,2,128]{5,4,1,2,0,3:T(2,128)(2,1)S(1)}, u32[]{:S(2)}, u32[]{:S(2)}) %all-to-all-start.1) | async-done | bytes 1179680 | tf_op jit(solution)/shard_map/all_to_all | solution.py:94
  124.4 3.2 %maximum_bitcast_fusion = bf16[6912,2,2,128]{3,0,2,1:T(8,128)(2,1)S(1)} fusion(bf16[1,2304,2,1,2,128]{5,1,4,2,3,0:T(8,128)(2,1)} %collective-permute-done.1, bf16[1,2304,2,1,2,128]{5,1,4,2,3,0:T(8,128)(2,1)S(1)} %bitcast.69, bf16[1,2304,2,1,2,128]{5,1,4,2,3,0:T(8,128)(2,1)} %collective-permute-done), kind=kLoop, calls=%fused_computation.38 | loop fusion | flops 21233664 | bytes 14155776 | tf_op jit(solution)/shard_map/reshape | solution.py:99
  128.0 5.4 %copy.37 = bf16[18,384,2,128]{3,2,1,0:T(2,128)(2,1)} copy(bf16[18,384,2,128]{3,1,0,2:T(8,128)(2,1)S(1)} %bitcast.66) | data formatting | bytes 7077888
  133.4 5.4 %copy.39 = bf16[18,384,2,128]{3,2,1,0:T(2,128)(2,1)} copy(bf16[18,384,2,128]{3,1,0,2:T(8,128)(2,1)S(1)} %bitcast.65) | data formatting | bytes 7077888
  138.9 132.1 %while.11 = (s32[]{:T(128)}, bf16[6,384,2,128]{3,2,1,0:T(2,128)(2,1)}, s32[6,7]{1,0:T(8,128)S(1)}, bf16[18,384,2,128]{3,2,1,0:T(2,128)(2,1)}, s32[6]{0:T(128)S(1...) while((s32[]{:T(128)}, ...), condition=%wide.region_3.5_spmd.clone, body=%wide.region_0.4_spmd.clone.sunk | while | flops 1081269376 | bytes 39746304 | solution.py:81
  138.9 5.3 %gather_fusion = bf16[7,384,2,128]{3,2,1,0:T(2,128)(2,1)S(1)} fusion(bf16[18,384,2,128]{3,2,1,0:T(2,128)(2,1)} %get-tuple-element.189, s32[1024]{0:T(1024)S(1)} %pad_clamp_fusion.2), kind=kCustom, calls=%fused_computation.clone.clone.1 | custom fusion | bytes 2752540 | tf_op jit(solution)/shard_map/while/body/eval_jaxpr/jit(_take)/gather | solution.py:65
  144.2 5.3 %gather_fusion.1 = bf16[7,384,2,128]{3,2,1,0:T(2,128)(2,1)S(1)} fusion(bf16[18,384,2,128]{3,2,1,0:T(2,128)(2,1)} %get-tuple-element.192, s32[1024]{0:T(1024)S(1)} %pad_clamp_fusion.2), kind=kCustom, calls=%fused_computation.1.clone.clone.1 | custom fusion | bytes 2752540 | tf_op jit(solution)/shard_map/while/body/eval_jaxpr/jit(_take)/gather | solution.py:64
  149.5 2.4 broadcast_select_fusion.3
  160.9 5.3 %gather_fusion = bf16[7,384,2,128]{3,2,1,0:T(2,128)(2,1)S(1)} fusion(bf16[18,384,2,128]{3,2,1,0:T(2,128)(2,1)} %get-tuple-element.189, s32[1024]{0:T(1024)S(1)} %pad_clamp_fusion.2), kind=kCustom, calls=%fused_computation.clone.clone.1 | custom fusion | bytes 2752540 | tf_op jit(solution)/shard_map/while/body/eval_jaxpr/jit(_take)/gather | solution.py:65
  166.2 5.3 %gather_fusion.1 = bf16[7,384,2,128]{3,2,1,0:T(2,128)(2,1)S(1)} fusion(bf16[18,384,2,128]{3,2,1,0:T(2,128)(2,1)} %get-tuple-element.192, s32[1024]{0:T(1024)S(1)} %pad_clamp_fusion.2), kind=kCustom, calls=%fused_computation.1.clone.clone.1 | custom fusion | bytes 2752540 | tf_op jit(solution)/shard_map/while/body/eval_jaxpr/jit(_take)/gather | solution.py:64
  171.6 2.4 broadcast_select_fusion.3
  182.9 5.3 %gather_fusion = bf16[7,384,2,128]{3,2,1,0:T(2,128)(2,1)S(1)} fusion(bf16[18,384,2,128]{3,2,1,0:T(2,128)(2,1)} %get-tuple-element.189, s32[1024]{0:T(1024)S(1)} %pad_clamp_fusion.2), kind=kCustom, calls=%fused_computation.clone.clone.1 | custom fusion | bytes 2752540 | tf_op jit(solution)/shard_map/while/body/eval_jaxpr/jit(_take)/gather | solution.py:65
  188.3 5.3 %gather_fusion.1 = bf16[7,384,2,128]{3,2,1,0:T(2,128)(2,1)S(1)} fusion(bf16[18,384,2,128]{3,2,1,0:T(2,128)(2,1)} %get-tuple-element.192, s32[1024]{0:T(1024)S(1)} %pad_clamp_fusion.2), kind=kCustom, calls=%fused_computation.1.clone.clone.1 | custom fusion | bytes 2752540 | tf_op jit(solution)/shard_map/while/body/eval_jaxpr/jit(_take)/gather | solution.py:64
  193.6 2.4 broadcast_select_fusion.3
  205.0 5.3 %gather_fusion = bf16[7,384,2,128]{3,2,1,0:T(2,128)(2,1)S(1)} fusion(bf16[18,384,2,128]{3,2,1,0:T(2,128)(2,1)} %get-tuple-element.189, s32[1024]{0:T(1024)S(1)} %pad_clamp_fusion.2), kind=kCustom, calls=%fused_computation.clone.clone.1 | custom fusion | bytes 2752540 | tf_op jit(solution)/shard_map/while/body/eval_jaxpr/jit(_take)/gather | solution.py:65
  210.3 5.3 %gather_fusion.1 = bf16[7,384,2,128]{3,2,1,0:T(2,128)(2,1)S(1)} fusion(bf16[18,384,2,128]{3,2,1,0:T(2,128)(2,1)} %get-tuple-element.192, s32[1024]{0:T(1024)S(1)} %pad_clamp_fusion.2), kind=kCustom, calls=%fused_computation.1.clone.clone.1 | custom fusion | bytes 2752540 | tf_op jit(solution)/shard_map/while/body/eval_jaxpr/jit(_take)/gather | solution.py:64
  215.6 2.4 broadcast_select_fusion.3
  227.0 5.3 %gather_fusion = bf16[7,384,2,128]{3,2,1,0:T(2,128)(2,1)S(1)} fusion(bf16[18,384,2,128]{3,2,1,0:T(2,128)(2,1)} %get-tuple-element.189, s32[1024]{0:T(1024)S(1)} %pad_clamp_fusion.2), kind=kCustom, calls=%fused_computation.clone.clone.1 | custom fusion | bytes 2752540 | tf_op jit(solution)/shard_map/while/body/eval_jaxpr/jit(_take)/gather | solution.py:65
  232.3 5.3 %gather_fusion.1 = bf16[7,384,2,128]{3,2,1,0:T(2,128)(2,1)S(1)} fusion(bf16[18,384,2,128]{3,2,1,0:T(2,128)(2,1)} %get-tuple-element.192, s32[1024]{0:T(1024)S(1)} %pad_clamp_fusion.2), kind=kCustom, calls=%fused_computation.1.clone.clone.1 | custom fusion | bytes 2752540 | tf_op jit(solution)/shard_map/while/body/eval_jaxpr/jit(_take)/gather | solution.py:64
  237.6 2.4 broadcast_select_fusion.3
  249.0 5.3 %gather_fusion = bf16[7,384,2,128]{3,2,1,0:T(2,128)(2,1)S(1)} fusion(bf16[18,384,2,128]{3,2,1,0:T(2,128)(2,1)} %get-tuple-element.189, s32[1024]{0:T(1024)S(1)} %pad_clamp_fusion.2), kind=kCustom, calls=%fused_computation.clone.clone.1 | custom fusion | bytes 2752540 | tf_op jit(solution)/shard_map/while/body/eval_jaxpr/jit(_take)/gather | solution.py:65
  254.3 5.3 %gather_fusion.1 = bf16[7,384,2,128]{3,2,1,0:T(2,128)(2,1)S(1)} fusion(bf16[18,384,2,128]{3,2,1,0:T(2,128)(2,1)} %get-tuple-element.192, s32[1024]{0:T(1024)S(1)} %pad_clamp_fusion.2), kind=kCustom, calls=%fused_computation.1.clone.clone.1 | custom fusion | bytes 2752540 | tf_op jit(solution)/shard_map/while/body/eval_jaxpr/jit(_take)/gather | solution.py:64
  259.7 2.4 broadcast_select_fusion.3
  271.0 3.1 %reshape_reshape_reshape_reshape_reshape.3 = bf16[8,2,144,1,256]{4,2,1,0,3:T(8,128)(2,1)S(1)} reshape(bf16[6,384,2,128]{3,2,1,0:T(2,128)(2,1)} %get-tuple-element.48) | data formatting | bytes 2359296 | tf_op jit(solution)/shard_map/reshape;reshape;reshape;reshape;reshape | solution.py:40
  274.2 4.8 %all_to_all.44 = bf16[8,2,144,1,256]{4,2,0,3,1:T(8,128)(2,1)S(1)} all-to-all(bf16[8,2,144,1,256]{4,2,0,3,1:T(8,128)(2,1)S(1)} %copy.41), channel_id=1, replica_groups=mesh['tm'=32,'head_0'=2,'head_1'=4,'head_2'=2] {'head_2'}, dimensions={1} | all-to-all | bytes 2359296 | tf_op jit(solution)/shard_map/all_to_all | solution.py:42
  279.1 21.3 %all_to_all.45 = bf16[8,2,144,1,256]{4,2,1,3,0:T(8,128)(2,1)S(1)} all-to-all(bf16[8,2,144,1,256]{4,2,1,3,0:T(8,128)(2,1)S(1)} %copy.42), channel_id=1, replica_groups=mesh['tm'=32,'head_0'=2,'head_1'=4,'head_2'=2] {'head_0','head_1'}, dimensions={0} | all-to-all | bytes 2359296 | tf_op jit(solution)/shard_map/all_to_all | solution.py:42
  (74 shorter events, 62.8 us)
Async XLA Ops:
  0.0 3.4 %copy-start = (bf16[144,4096]{1,0:T(8,128)(2,1)S(1)}, bf16[144,4096]{1,0:T(8,128)(2,1)}, u32[]{:S(2)}) copy-start(bf16[144,4096]{1,0:T(8,128)(2,1)} %param.10) | copy-start | bytes 3538948
  49.1 75.2 %collective-permute-start = (bf16[1,2304,2,1,2,128]{5,1,4,2,3,0:T(8,128)(2,1)S(1)}, bf16[1,2304,2,1,2,128]{5,1,4,2,3,0:T(8,128)(2,1)}, u32[]{:S(2)}, u32[]{:S(2)}) collective-permute-start(bf16[1,2304,2,1,2,128]{5,1,4,2,3,0:T(8,128)(2,1)S(1)} %bitcast.67), channel_id=1, source_target_pairs={{0,16},{16,32},{32,48},{48,64},{64,80},{80,96},{96,112},{112,128},... | collective-permute-start | bytes 7077896 | tf_op jit(solution)/shard_map/ppermute | solution.py:18
  51.9 72.5 %collective-permute-start.1 = (bf16[1,2304,2,1,2,128]{5,1,4,2,3,0:T(8,128)(2,1)S(1)}, bf16[1,2304,2,1,2,128]{5,1,4,2,3,0:T(8,128)(2,1)}, u32[]{:S(2)}, u32[]{:S(2)}) collective-permute-start(bf16[1,2304,2,1,2,128]{5,1,4,2,3,0:T(8,128)(2,1)S(1)} %bitcast.68), channel_id=1, source_target_pairs={{16,0},{32,16},{48,32},{64,48},{80,64},{96,80},{112,96},{128,112},... | collective-permute-start | bytes 7077896 | tf_op jit(solution)/shard_map/ppermute | solution.py:21
  56.5 6.4 %copy-start.1 = (s32[6,7]{1,0:T(8,128)S(1)}, s32[6,7]{1,0:T(8,128)}, u32[]{:S(2)}) copy-start(s32[6,7]{1,0:T(8,128)} %param.12) | copy-start | bytes 508
  58.4 64.8 %all-to-all-start.1 = ((bf16[1,144,1,16,2,128]{5,4,1,2,0,3:T(2,128)(2,1)}), bf16[1,144,1,16,2,128]{5,4,1,2,0,3:T(2,128)(2,1)S(1)}, u32[]{:S(2)}, u32[]{:S(2)}) async-start(bf16[1,144,1,16,2,128]{5,4,1,2,0,3:T(2,128)(2,1)} %copy.35), calls=%async_computation.1 | async-start | bytes 2359296 | tf_op jit(solution)/shard_map/all_to_all | solution.py:94
  133.4 5.5 %copy-start.2 = (s32[6]{0:T(128)S(1)}, s32[6]{0:T(128)}, u32[]{:S(2)}) copy-start(s32[6]{0:T(128)} %param.13) | copy-start | bytes 76
where the time goes:
time: 303 us; the launch traced here: 302 us
  local copies, waits for them, and re-layouts  102 us (34%)
  blocking collectives  65.1 us (21%)
  waiting for transfers between devices  60.3 us (20%)
  other arithmetic  36.3 us (12%)
  matrix products  28.9 us (10%)
  starting transfers between devices  8.47 us (3%)
    all_to_all x1, waiting for transfers between devices, shards(): lax.all_to_all(query_six, HEAD, split_axis=3, concat_axis=1, tiled=True)  60.3 us
    all_to_all x1, blocking collectives, shards(): lax.all_to_all(paired, HEAD, split_axis=3, concat_axis=1, tiled=True)  39 us
    gather x6, local copies, waits for them, and re-layouts, per_tile(): jnp.take(key_tiles, listed, axis=0).reshape(key_span, head_count, HD)  31.9 us
    gather x6, local copies, waits for them, and re-layouts, per_tile(): jnp.take(value_tiles, listed, axis=0).reshape(key_span, head_count, HD)  31.9 us
    all_to_all x2, blocking collectives, moved_by_axis(): lax.all_to_all(blocks, axes[k], split_axis=k, concat_axis=k, tiled=True)  26.1 us
    select_n x6, other arithmetic, per_tile(): jnp.take(value_tiles, listed, axis=0).reshape(key_span, head_count, HD)  14.6 us
    dot_general x6, matrix products, per_tile(): jnp.einsum('qhd,khd->hqk', query_tile, key_block, preferred_element_type=...  14.6 us
    dot_general x6, matrix products, per_tile(): jnp.einsum('hqk,khd->qhd', weights, value_block, preferred_element_type=j...  14.4 us
  transfers between devices with their start and end apart: 3, of which 1 were waited for; matrix products, arithmetic and copies ran while one was open for 2% of the time, Pallas kernels for 0%

commit v1 on v0

v1 whole, which is shorter than its diff:
```python
import functools

import jax
import jax.numpy as jnp
from jax import lax
from jax.experimental import pallas as pl
from jax.experimental.pallas import tpu as pltpu
from jax.sharding import PartitionSpec as P

HD = 128
TILE = 384
BLOCK = 48
PER_TILE = TILE // BLOCK
LOG2E = 1.4426950408889634
NT = (((1,), (1,)), ((), ()))
MESH = pl.DeviceIdType.MESH


def tile_of(ref, first_block):
    return ref[pl.ds(first_block, PER_TILE)].reshape(TILE, HD)


def tile_attention(query, key_ref, value_ref, starts, biases, scale, score_ref):
    slots = len(starts)
    highest = None
    for s in range(slots):
        key_tile = tile_of(key_ref, starts[s])
        score = lax.dot_general(query, key_tile, NT, preferred_element_type=jnp.float32)
        score_ref[:, s * TILE : (s + 1) * TILE] = score
    for s in range(slots):
        score = score_ref[:, s * TILE : (s + 1) * TILE]
        top = jnp.max(score, axis=1, keepdims=True) * scale + biases[s]
        highest = top if highest is None else jnp.maximum(highest, top)
    total = jnp.zeros((TILE, 1), jnp.float32)
    summed = jnp.zeros((TILE, HD), jnp.float32)
    for s in range(slots):
        score = score_ref[:, s * TILE : (s + 1) * TILE]
        raised = jnp.exp2(score * scale - (highest - biases[s]))
        total += jnp.sum(raised, axis=1, keepdims=True)
        value_tile = tile_of(value_ref, starts[s])
        summed += jnp.dot(
            raised.astype(jnp.bfloat16), value_tile, preferred_element_type=jnp.float32
        )
    return summed * (1.0 / total)


def kernel(
    n_tm, half, group, tiles, slots,
    list_ref, count_ref, q_ref, k_ref, v_ref, o_ref,
    qa, ka, va, qb, kb, vb, oa, ob, score_ref,
    own_sem, send_sem, recv_sem, zsend_sem, zrecv_sem, osend_sem, orecv_sem, oown_sem,
):
    tok = q_ref.shape[0]
    slab = group * tok
    tm = lax.axis_index("tm")
    me = lax.axis_index("head")
    mirror = (group // 2) * (tm // half)
    mine = lax.rem(me + mirror, group)
    up_tm = lax.rem(tm + 1, n_tm)
    down_tm = lax.rem(tm + n_tm - 1, n_tm)
    up = (up_tm, lax.rem(mine + (group // 2) * (up_tm // half), group))
    down = (down_tm, lax.rem(mine + (group // 2) * (down_tm // half), group))

    sources = (k_ref, v_ref, q_ref)
    parts = {
        "ka": (ka, k_ref, 0, slab, 0),
        "va": (va, v_ref, 0, slab, 1),
        "kb": (kb, k_ref, 1, slab, 2),
        "vb": (vb, v_ref, 1, slab, 3),
        "qa": (qa, q_ref, 0, 0, 4),
        "qb": (qb, q_ref, 1, 0, 5),
    }

    def columns(owner, head):
        return pl.ds(pl.multiple_of(owner * (2 * HD) + head * HD, HD), HD)

    def rows(first, device):
        return pl.ds(first + device * tok, tok)

    def own_copy(name):
        buf, src, head, first, t = parts[name]
        return pltpu.make_async_copy(
            src.at[:, :, columns(mine, head)], buf.at[rows(first, me)], own_sem.at[t]
        )

    def spread(name):
        buf, src, head, first, t = parts[name]

        def step(d, carry):
            peer = lax.rem(me + d, group)
            pltpu.make_async_remote_copy(
                src_ref=src.at[:, :, columns(lax.rem(peer + mirror, group), head)],
                dst_ref=buf.at[rows(first, me)],
                send_sem=send_sem.at[t],
                recv_sem=recv_sem.at[t, me],
                device_id=(tm, peer),
                device_id_type=MESH,
            ).start()
            return carry

        lax.fori_loop(1, group, step, 0)

    def arrived(name, source):
        buf, _, _, first, t = parts[name]
        pltpu.make_async_copy(
            buf.at[rows(first, source)], buf.at[rows(first, source)], recv_sem.at[t, source]
        ).wait()

    def to_halo(name, source):
        buf, _, _, first, t = parts[name]
        for way, device, landing in ((0, up, 0), (1, down, 2 * slab)):
            pltpu.make_async_remote_copy(
                src_ref=buf.at[rows(first, source)],
                dst_ref=buf.at[rows(landing, source)],
                send_sem=zsend_sem.at[t, way],
                recv_sem=zrecv_sem.at[t, way],
                device_id=device,
                device_id_type=MESH,
            ).start()

    def forward(name):
        own_copy(name).wait()
        to_halo(name, me)

        def step(d, carry):
            source = lax.rem(me + group - d, group)
            arrived(name, source)
            to_halo(name, source)
            return carry

        lax.fori_loop(1, group, step, 0)

    def gather(name):
        own_copy(name).wait()

        def step(d, carry):
            arrived(name, lax.rem(me + group - d, group))
            return carry

        lax.fori_loop(1, group, step, 0)

    def halo_wait(name, sems):
        buf, _, _, _, t = parts[name]
        for way in range(2):
            whole = buf.at[pl.ds(0, slab)]
            pltpu.make_async_copy(whole, whole, sems.at[t, way]).wait()

    def return_rows(out_buf, head, device):
        @pl.when(device != me)
        def _():
            pltpu.make_async_remote_copy(
                src_ref=out_buf.at[rows(0, device)],
                dst_ref=o_ref.at[:, :, columns(mine, head)],
                send_sem=osend_sem.at[head],
                recv_sem=orecv_sem.at[head],
                device_id=(tm, device),
                device_id_type=MESH,
            ).start()

        @pl.when(device == me)
        def _():
            pltpu.make_async_copy(
                out_buf.at[rows(0, device)], o_ref.at[:, :, columns(mine, head)], oown_sem.at[head]
            ).start()

    scale = HD ** (-0.5) * LOG2E

    def attend(names, out_buf, head, between=None):
        query_buf, key_buf, value_buf = (parts[n][0] for n in names)

        def step(i, carry):
            if between is not None:
                pl.when(i == tiles // 2)(between)
            starts = [
                jnp.clip(list_ref[i, s] - (tm - 1) * tiles, 0, 3 * tiles - 1) * PER_TILE
                for s in range(slots)
            ]
            count = count_ref[i]
            biases = [
                (jnp.minimum(count - s, 1) - 1).astype(jnp.float32) * 1e30 for s in range(slots)
            ]
            result = tile_attention(
                tile_of(query_buf, i * PER_TILE), key_buf, value_buf, starts, biases, scale, score_ref
            )
            out_buf[pl.ds(i * PER_TILE, PER_TILE)] = result.astype(out_buf.dtype).reshape(
                PER_TILE, BLOCK, HD
            )

            def send(device, carry):
                return_rows(out_buf, head, device)
                return carry

            lax.fori_loop((i * PER_TILE) // tok, ((i + 1) * PER_TILE) // tok, send, 0)
            return carry

        lax.fori_loop(0, tiles, step, 0)

    order = ("ka", "va", "kb", "qa", "vb", "qb")
    for name in order:
        own_copy(name).start()

    barrier = pltpu.get_barrier_semaphore()

    def greet(d, carry):
        pl.semaphore_signal(
            barrier, inc=1, device_id=(tm, lax.rem(me + d, group)), device_id_type=MESH
        )
        return carry

    lax.fori_loop(1, group, greet, 0)
    for device in (up, down):
        pl.semaphore_signal(barrier, inc=1, device_id=device, device_id_type=MESH)
    pl.semaphore_wait(barrier, group + 1)

    for name in order:
        spread(name)
    forward("ka")
    forward("va")
    forward("kb")
    gather("qa")
    for name in ("ka", "va"):
        halo_wait(name, zrecv_sem)
    attend(("qa", "ka", "va"), oa, 0, lambda: forward("vb"))
    gather("qb")
    for name in ("kb", "vb"):
        halo_wait(name, zrecv_sem)
    attend(("qb", "kb", "vb"), ob, 1)

    for name in order:
        buf, _, _, first, t = parts[name]
        sent = buf.at[pl.ds(first, (group - 1) * tok)]
        pltpu.make_async_copy(sent, sent, send_sem.at[t]).wait()
    for name in ("ka", "va", "kb", "vb"):
        halo_wait(name, zsend_sem)
    for head, out_buf in enumerate((oa, ob)):
        others = out_buf.at[pl.ds(0, (group - 1) * tok)]
        pltpu.make_async_copy(others, others, osend_sem.at[head]).wait()
        pltpu.make_async_copy(others, others, orecv_sem.at[head]).wait()
        pltpu.make_async_copy(
            out_buf.at[rows(0, me)], o_ref.at[:, :, columns(mine, head)], oown_sem.at[head]
        ).wait()


def shards(queries, keys, values, tile_list, tile_count):
    n_tm, group = lax.axis_size("tm"), lax.axis_size("head")
    rows, width = queries.shape
    tok = rows // BLOCK
    slab = group * tok
    tiles, slots = tile_list.shape
    smem = pl.BlockSpec(memory_space=pltpu.SMEM)
    anywhere = pl.BlockSpec(memory_space=pl.ANY)
    narrow = pltpu.VMEM((slab, BLOCK, HD), jnp.bfloat16)
    wide = pltpu.VMEM((3 * slab, BLOCK, HD), jnp.bfloat16)
    dma = pltpu.SemaphoreType.DMA
    out = pl.pallas_call(
        functools.partial(kernel, n_tm, n_tm // 2, group, tiles, slots),
        out_shape=jax.ShapeDtypeStruct((tok, BLOCK, width), queries.dtype),
        in_specs=[smem, smem, anywhere, anywhere, anywhere],
        out_specs=anywhere,
        scratch_shapes=[
            narrow, wide, wide, narrow, wide, wide, narrow, narrow,
            pltpu.VMEM((TILE, slots * TILE), jnp.float32),
            dma((6,)), dma((6,)), dma((6, group)), dma((4, 2)), dma((4, 2)),
            dma((2,)), dma((2,)), dma((2,)),
        ],
        compiler_params=pltpu.CompilerParams(
            collective_id=0, has_side_effects=True, vmem_limit_bytes=48 * 2**20
        ),
    )(tile_list, tile_count, *(x.reshape(tok, BLOCK, width) for x in (queries, keys, values)))
    return out.reshape(rows, width)


def solution(mesh):
    by_token, by_tile = P(("tm", "head"), None), P("tm", None)
    return jax.shard_map(
        shards,
        mesh=mesh,
        in_specs=(by_token, by_token, by_token, by_tile, P("tm")),
        out_specs=by_token,
        check_vma=False,
    )
```

time: 303 us -> 97.2 us (0.32)
  the two profiles are of different devices: /device:TPU:1 before, /device:TPU:27 now
where the time goes in v1:
time: 97.2 us; the launch traced here: 97 us
  Pallas kernels  90.8 us (93%)
  local copies, waits for them, and re-layouts  6.17 us (6%)
    pallas_call x1, Pallas kernels, shards(): pl.pallas_call(functools.partial(kernel, n_tm, n_tm // 2, group, tiles, s...  90.8 us
    unnamed x11, local copies, waits for them, and re-layouts  6.17 us

profile of v1, /device:TPU:27, one launch (start us, length us, event | category | flops | bytes accessed | tf_op | source)
XLA Modules:
  0.0 97.0 jit_solution(4048531888346982324)
XLA Ops:
  0.0 0.0 copy-start
  0.0 1.3 %copy-done = bf16[144,4096]{1,0:T(8,128)(2,1)S(1)} copy-done((bf16[144,4096]{1,0:T(8,128)(2,1)S(1)}, bf16[144,4096]{1,0:T(8,128)(2,1)}, u32[]{:S(2)}) %copy-start) | copy-done | bytes 1179672
  1.3 0.0 copy-start.1
  1.3 1.3 %copy-done.1 = bf16[144,4096]{1,0:T(8,128)(2,1)S(1)} copy-done((bf16[144,4096]{1,0:T(8,128)(2,1)S(1)}, bf16[144,4096]{1,0:T(8,128)(2,1)}, u32[]{:S(2)}) %copy-start.1) | copy-done | bytes 1179672
  2.5 0.0 copy-start.2
  2.5 1.3 %copy-done.2 = bf16[144,4096]{1,0:T(8,128)(2,1)S(1)} copy-done((bf16[144,4096]{1,0:T(8,128)(2,1)S(1)}, bf16[144,4096]{1,0:T(8,128)(2,1)}, u32[]{:S(2)}) %copy-start.2) | copy-done | bytes 1179672
  3.8 0.0 copy-start.3
  3.8 0.7 copy-done.3
  4.5 0.0 copy-start.4
  4.5 0.7 copy-done.4
  5.2 90.8 %shard_map.55 = bf16[3,48,4096]{2,1,0:T(8,128)(2,1)S(1)} custom-call(s32[6,7]{1,0:T(8,128)S(1)} %copy-done.3, s32[6]{0:T(128)S(1)} %copy-done.4, bf16[3,48,4096]{2,1,0:T(8,128)(2,1)S(1)} %bitcast.5, bf16[3,48,4096]{2,1,0:T(8,128)(2,1)S(1)} %bitcast.6, bf16[3,48,4096]{2,1,0:T(8,128)(2,1)S(1)} %bitcast.7), custom_call_target="tpu_custom_call" | custom-call | tf_op jit(solution)/shard_map/pallas_call | solution.py:255
  95.9 1.0 %copy.7 = bf16[144,4096]{1,0:T(8,128)(2,1)} copy(bf16[144,4096]{1,0:T(8,128)(2,1)S(1)} %bitcast.4) | data formatting | bytes 2359296
Async XLA Ops:
  0.0 1.3 %copy-start = (bf16[144,4096]{1,0:T(8,128)(2,1)S(1)}, bf16[144,4096]{1,0:T(8,128)(2,1)}, u32[]{:S(2)}) copy-start(bf16[144,4096]{1,0:T(8,128)(2,1)} %param.5) | copy-start | bytes 3538948
  1.3 1.3 %copy-start.1 = (bf16[144,4096]{1,0:T(8,128)(2,1)S(1)}, bf16[144,4096]{1,0:T(8,128)(2,1)}, u32[]{:S(2)}) copy-start(bf16[144,4096]{1,0:T(8,128)(2,1)} %param.6) | copy-start | bytes 3538948
  2.5 1.3 %copy-start.2 = (bf16[144,4096]{1,0:T(8,128)(2,1)S(1)}, bf16[144,4096]{1,0:T(8,128)(2,1)}, u32[]{:S(2)}) copy-start(bf16[144,4096]{1,0:T(8,128)(2,1)} %param.7) | copy-start | bytes 3538948
  3.8 0.7 copy-start.3
  4.5 0.7 copy-start.4

commit v2 on v1

--- a/solution.py
+++ b/solution.py
@@ -20,34 +20,64 @@
     return ref[pl.ds(first_block, PER_TILE)].reshape(TILE, HD)
 
 
+def score_tiles(query, key_ref, starts, biases, scale, score_ref):
+    highest = None
+    for s, start in enumerate(starts):
+        key_tile = tile_of(key_ref, start)
+        score_ref[:, s * TILE : (s + 1) * TILE] = lax.dot_general(
+            query, key_tile, NT, preferred_element_type=jnp.float32
+        )
+    for s, bias in enumerate(biases):
+        score = score_ref[:, s * TILE : (s + 1) * TILE]
+        top = jnp.max(score, axis=1, keepdims=True) * scale + bias
+        highest = top if highest is None else jnp.maximum(highest, top)
+    return highest
+
+
+def raised_tile(score_ref, s, scale, highest, bias):
+    return jnp.exp2(score_ref[:, s * TILE : (s + 1) * TILE] * scale - (highest - bias))
+
+
 def tile_attention(query, key_ref, value_ref, starts, biases, scale, score_ref):
-    slots = len(starts)
-    highest = None
-    for s in range(slots):
-        key_tile = tile_of(key_ref, starts[s])
-        score = lax.dot_general(query, key_tile, NT, preferred_element_type=jnp.float32)
-        score_ref[:, s * TILE : (s + 1) * TILE] = score
-    for s in range(slots):
-        score = score_ref[:, s * TILE : (s + 1) * TILE]
-        top = jnp.max(score, axis=1, keepdims=True) * scale + biases[s]
-        highest = top if highest is None else jnp.maximum(highest, top)
+    highest = score_tiles(query, key_ref, starts, biases, scale, score_ref)
     total = jnp.zeros((TILE, 1), jnp.float32)
     summed = jnp.zeros((TILE, HD), jnp.float32)
-    for s in range(slots):
-        score = score_ref[:, s * TILE : (s + 1) * TILE]
-        raised = jnp.exp2(score * scale - (highest - biases[s]))
+    for s, start in enumerate(starts):
+        raised = raised_tile(score_ref, s, scale, highest, biases[s])
         total += jnp.sum(raised, axis=1, keepdims=True)
-        value_tile = tile_of(value_ref, starts[s])
         summed += jnp.dot(
-            raised.astype(jnp.bfloat16), value_tile, preferred_element_type=jnp.float32
+            raised.astype(jnp.bfloat16),
+            tile_of(value_ref, start),
+            preferred_element_type=jnp.float32,
         )
     return summed * (1.0 / total)
+
+
+def tile_weights(query, key_ref, starts, biases, scale, score_ref, weight_ref, i):
+    highest = score_tiles(query, key_ref, starts, biases, scale, score_ref)
+    total = jnp.zeros((TILE, 1), jnp.float32)
+    for s, bias in enumerate(biases):
+        raised = raised_tile(score_ref, s, scale, highest, bias)
+        total += jnp.sum(raised, axis=1, keepdims=True)
+        weight_ref[i, :, s * TILE : (s + 1) * TILE] = raised.astype(jnp.bfloat16)
+    return 1.0 / total
+
+
+def weighted_sum(value_ref, starts, weight_ref, i):
+    summed = jnp.zeros((TILE, HD), jnp.float32)
+    for s, start in enumerate(starts):
+        summed += jnp.dot(
+            weight_ref[i, :, s * TILE : (s + 1) * TILE],
+            tile_of(value_ref, start),
+            preferred_element_type=jnp.float32,
+        )
+    return summed
 
 
 def kernel(
     n_tm, half, group, tiles, slots,
     list_ref, count_ref, q_ref, k_ref, v_ref, o_ref,
-    qa, ka, va, qb, kb, vb, oa, ob, score_ref,
+    qa, ka, va, qb, kb, vb, oa, ob, score_ref, weight_ref, inverse_ref,
     own_sem, send_sem, recv_sem, zsend_sem, zrecv_sem, osend_sem, orecv_sem, oown_sem,
 ):
     tok = q_ref.shape[0]
@@ -119,9 +149,6 @@
             ).start()
 
     def forward(name):
-        own_copy(name).wait()
-        to_halo(name, me)
-
         def step(d, carry):
             source = lax.rem(me + group - d, group)
             arrived(name, source)
@@ -165,35 +192,48 @@
 
     scale = HD ** (-0.5) * LOG2E
 
-    def attend(names, out_buf, head, between=None):
-        query_buf, key_buf, value_buf = (parts[n][0] for n in names)
-
-        def step(i, carry):
-            if between is not None:
-                pl.when(i == tiles // 2)(between)
-            starts = [
-                jnp.clip(list_ref[i, s] - (tm - 1) * tiles, 0, 3 * tiles - 1) * PER_TILE
-                for s in range(slots)
-            ]
-            count = count_ref[i]
-            biases = [
-                (jnp.minimum(count - s, 1) - 1).astype(jnp.float32) * 1e30 for s in range(slots)
-            ]
-            result = tile_attention(
-                tile_of(query_buf, i * PER_TILE), key_buf, value_buf, starts, biases, scale, score_ref
-            )
-            out_buf[pl.ds(i * PER_TILE, PER_TILE)] = result.astype(out_buf.dtype).reshape(
-                PER_TILE, BLOCK, HD
-            )
-
-            def send(device, carry):
-                return_rows(out_buf, head, device)
-                return carry
-
-            lax.fori_loop((i * PER_TILE) // tok, ((i + 1) * PER_TILE) // tok, send, 0)
+    def starts_of(i):
+        return [
+            jnp.clip(list_ref[i, s] - (tm - 1) * tiles, 0, 3 * tiles - 1) * PER_TILE
+            for s in range(slots)
+        ]
+
+    def biases_of(i):
+        return [
+            (jnp.minimum(count_ref[i] - s, 1) - 1).astype(jnp.float32) * 1e30
+            for s in range(slots)
+        ]
+
+    def finish(out_buf, head, i, result):
+        out_buf[pl.ds(i * PER_TILE, PER_TILE)] = result.astype(out_buf.dtype).reshape(
+            PER_TILE, BLOCK, HD
+        )
+
+        def send(device, carry):
+            return_rows(out_buf, head, device)
             return carry
 
-        lax.fori_loop(0, tiles, step, 0)
+        lax.fori_loop((i * PER_TILE) // tok, ((i + 1) * PER_TILE) // tok, send, 0)
+
+    def first_head(i, carry):
+        pl.when(i == tiles // 2)(lambda: forward("vb"))
+        result = tile_attention(
+            tile_of(qa, i * PER_TILE), ka, va, starts_of(i), biases_of(i), scale, score_ref
+        )
+        finish(oa, 0, i, result)
+        return carry
+
+    def second_weights(i, carry):
+        inverse_ref[i] = tile_weights(
+            tile_of(qb, i * PER_TILE), kb, starts_of(i), biases_of(i), scale, score_ref,
+            weight_ref, i,
+        )
+        return carry
+
+    def second_head(i, carry):
+        result = weighted_sum(vb, starts_of(i), weight_ref, i) * inverse_ref[i]
+        finish(ob, 1, i, result)
+        return carry
 
     order = ("ka", "va", "kb", "qa", "vb", "qb")
     for name in order:
@@ -212,19 +252,23 @@
         pl.semaphore_signal(barrier, inc=1, device_id=device, device_id_type=MESH)
     pl.semaphore_wait(barrier, group + 1)
 
+    for name in ("ka", "va", "kb", "vb"):
+        own_copy(name).wait()
+        to_halo(name, me)
     for name in order:
         spread(name)
     forward("ka")
     forward("va")
     forward("kb")
     gather("qa")
-    for name in ("ka", "va"):
-        halo_wait(name, zrecv_sem)
-    attend(("qa", "ka", "va"), oa, 0, lambda: forward("vb"))
+    halo_wait("ka", zrecv_sem)
+    halo_wait("va", zrecv_sem)
+    lax.fori_loop(0, tiles, first_head, 0)
     gather("qb")
-    for name in ("kb", "vb"):
-        halo_wait(name, zrecv_sem)
-    attend(("qb", "kb", "vb"), ob, 1)
+    halo_wait("kb", zrecv_sem)
+    lax.fori_loop(0, tiles, second_weights, 0)
+    halo_wait("vb", zrecv_sem)
+    lax.fori_loop(0, tiles, second_head, 0)
 
     for name in order:
         buf, _, _, first, t = parts[name]
@@ -260,11 +304,13 @@
         scratch_shapes=[
             narrow, wide, wide, narrow, wide, wide, narrow, narrow,
             pltpu.VMEM((TILE, slots * TILE), jnp.float32),
+            pltpu.VMEM((tiles, TILE, slots * TILE), jnp.bfloat16),
+            pltpu.VMEM((tiles, TILE, 1), jnp.float32),
             dma((6,)), dma((6,)), dma((6, group)), dma((4, 2)), dma((4, 2)),
             dma((2,)), dma((2,)), dma((2,)),
         ],
         compiler_params=pltpu.CompilerParams(
-            collective_id=0, has_side_effects=True, vmem_limit_bytes=48 * 2**20
+            collective_id=0, has_side_effects=True, vmem_limit_bytes=60 * 2**20
         ),
     )(tile_list, tile_count, *(x.reshape(tok, BLOCK, width) for x in (queries, keys, values)))
     return out.reshape(rows, width)

time: 97.2 us -> 85.5 us (0.88)
  Pallas kernels: 90.8 us -> 82.9 us
  local copies, waits for them, and re-layouts: 6.17 us -> 2.39 us
    pallas_call x1, Pallas kernels: 90.8 us -> 82.9 us  [shards(): pl.pallas_call(functools.partial(kernel, n_tm, n_tm // 2, group, tiles, s...]
    unnamed x11 -> x1, local copies, waits for them, and re-layouts: 6.17 us -> 2.39 us
where the time goes in v2:
time: 85.5 us; the launch traced here: 85.3 us
  Pallas kernels  82.9 us (97%)
  local copies, waits for them, and re-layouts  2.39 us (3%)
    pallas_call x1, Pallas kernels, shards(): pl.pallas_call(functools.partial(kernel, n_tm, n_tm // 2, group, tiles, s...  82.9 us
    unnamed x1, local copies, waits for them, and re-layouts  2.39 us

profile of v2, /device:TPU:27, one launch (start us, length us, event | category | flops | bytes accessed | tf_op | source)
XLA Modules:
  0.0 85.3 jit_solution(13041910994763393116)
XLA Ops:
  0.0 82.9 %shard_map.55 = bf16[3,48,4096]{2,1,0:T(8,128)(2,1)} custom-call(s32[6,7]{1,0:T(8,128)} %list_ref.1, s32[6]{0:T(128)} %count_ref.1, bf16[3,48,4096]{2,1,0:T(8,128)(2,1)} %bitcast.5, bf16[3,48,4096]{2,1,0:T(8,128)(2,1)} %bitcast.6, bf16[3,48,4096]{2,1,0:T(8,128)(2,1)} %bitcast.7), custom_call_target="tpu_custom_call" | custom-call | tf_op jit(solution)/shard_map/pallas_call | solution.py:299
  82.9 2.4 %copy.7 = bf16[144,4096]{1,0:T(8,128)(2,1)} copy(bf16[144,4096]{1,0:T(8,128)(2,1)} %bitcast.4) | data formatting | bytes 2359296

commit v3 on v2

--- a/solution.py
+++ b/solution.py
@@ -91,7 +91,6 @@
     up = (up_tm, lax.rem(mine + (group // 2) * (up_tm // half), group))
     down = (down_tm, lax.rem(mine + (group // 2) * (down_tm // half), group))
 
-    sources = (k_ref, v_ref, q_ref)
     parts = {
         "ka": (ka, k_ref, 0, slab, 0),
         "va": (va, v_ref, 0, slab, 1),
@@ -138,15 +137,21 @@
 
     def to_halo(name, source):
         buf, _, _, first, t = parts[name]
-        for way, device, landing in ((0, up, 0), (1, down, 2 * slab)):
-            pltpu.make_async_remote_copy(
-                src_ref=buf.at[rows(first, source)],
-                dst_ref=buf.at[rows(landing, source)],
-                send_sem=zsend_sem.at[t, way],
-                recv_sem=zrecv_sem.at[t, way],
-                device_id=device,
-                device_id_type=MESH,
-            ).start()
+        for way, device, there, landing in (
+            (0, up, tm < n_tm - 1, 0),
+            (1, down, tm > 0, 2 * slab),
+        ):
+
+            @pl.when(there)
+            def _(way=way, device=device, landing=landing):
+                pltpu.make_async_remote_copy(
+                    src_ref=buf.at[rows(first, source)],
+                    dst_ref=buf.at[rows(landing, source)],
+                    send_sem=zsend_sem.at[t, way],
+                    recv_sem=zrecv_sem.at[t, way],
+                    device_id=device,
+                    device_id_type=MESH,
+                ).start()
 
     def forward(name):
         def step(d, carry):
@@ -166,18 +171,25 @@
 
         lax.fori_loop(1, group, step, 0)
 
-    def halo_wait(name, sems):
+    def halo_wait(name, sems, low_way):
         buf, _, _, _, t = parts[name]
-        for way in range(2):
-            whole = buf.at[pl.ds(0, slab)]
-            pltpu.make_async_copy(whole, whole, sems.at[t, way]).wait()
-
-    def return_rows(out_buf, head, device):
+        for way, there in ((low_way, tm > 0), (1 - low_way, tm < n_tm - 1)):
+
+            @pl.when(there)
+            def _(way=way):
+                whole = buf.at[pl.ds(0, slab)]
+                pltpu.make_async_copy(whole, whole, sems.at[t, way]).wait()
+
+    def return_block(out_buf, head, block):
+        device = block // tok
+        src = out_buf.at[pl.ds(block, 1)]
+        dst = o_ref.at[pl.ds(block - device * tok, 1), :, columns(mine, head)]
+
         @pl.when(device != me)
         def _():
             pltpu.make_async_remote_copy(
-                src_ref=out_buf.at[rows(0, device)],
-                dst_ref=o_ref.at[:, :, columns(mine, head)],
+                src_ref=src,
+                dst_ref=dst,
                 send_sem=osend_sem.at[head],
                 recv_sem=orecv_sem.at[head],
                 device_id=(tm, device),
@@ -186,9 +198,7 @@
 
         @pl.when(device == me)
         def _():
-            pltpu.make_async_copy(
-                out_buf.at[rows(0, device)], o_ref.at[:, :, columns(mine, head)], oown_sem.at[head]
-            ).start()
+            pltpu.make_async_copy(src, dst, oown_sem.at[head]).start()
 
     scale = HD ** (-0.5) * LOG2E
 
@@ -209,14 +219,17 @@
             PER_TILE, BLOCK, HD
         )
 
-        def send(device, carry):
-            return_rows(out_buf, head, device)
+        def send(b, carry):
+            return_block(out_buf, head, i * PER_TILE + b)
             return carry
 
-        lax.fori_loop((i * PER_TILE) // tok, ((i + 1) * PER_TILE) // tok, send, 0)
-
-    def first_head(i, carry):
-        pl.when(i == tiles // 2)(lambda: forward("vb"))
+        lax.fori_loop(0, PER_TILE, send, 0)
+
+    begin = (me * tiles) // group
+
+    def first_head(j, carry):
+        pl.when(j == tiles // 2)(lambda: forward("vb"))
+        i = lax.rem(begin + j, tiles)
         result = tile_attention(
             tile_of(qa, i * PER_TILE), ka, va, starts_of(i), biases_of(i), scale, score_ref
         )
@@ -230,7 +243,8 @@
         )
         return carry
 
-    def second_head(i, carry):
+    def second_head(j, carry):
+        i = lax.rem(begin + j, tiles)
         result = weighted_sum(vb, starts_of(i), weight_ref, i) * inverse_ref[i]
         finish(ob, 1, i, result)
         return carry
@@ -248,9 +262,14 @@
         return carry
 
     lax.fori_loop(1, group, greet, 0)
-    for device in (up, down):
-        pl.semaphore_signal(barrier, inc=1, device_id=device, device_id_type=MESH)
-    pl.semaphore_wait(barrier, group + 1)
+    for device, there in ((up, tm < n_tm - 1), (down, tm > 0)):
+
+        @pl.when(there)
+        def _(device=device):
+            pl.semaphore_signal(barrier, inc=1, device_id=device, device_id_type=MESH)
+
+    beside = jnp.minimum(tm, 1) + jnp.minimum(n_tm - 1 - tm, 1)
+    pl.semaphore_wait(barrier, group - 1 + beside)
 
     for name in ("ka", "va", "kb", "vb"):
         own_copy(name).wait()
@@ -261,13 +280,13 @@
     forward("va")
     forward("kb")
     gather("qa")
-    halo_wait("ka", zrecv_sem)
-    halo_wait("va", zrecv_sem)
+    halo_wait("ka", zrecv_sem, 0)
+    halo_wait("va", zrecv_sem, 0)
     lax.fori_loop(0, tiles, first_head, 0)
     gather("qb")
-    halo_wait("kb", zrecv_sem)
+    halo_wait("kb", zrecv_sem, 0)
     lax.fori_loop(0, tiles, second_weights, 0)
-    halo_wait("vb", zrecv_sem)
+    halo_wait("vb", zrecv_sem, 0)
     lax.fori_loop(0, tiles, second_head, 0)
 
     for name in order:
@@ -275,7 +294,7 @@
         sent = buf.at[pl.ds(first, (group - 1) * tok)]
         pltpu.make_async_copy(sent, sent, send_sem.at[t]).wait()
     for name in ("ka", "va", "kb", "vb"):
-        halo_wait(name, zsend_sem)
+        halo_wait(name, zsend_sem, 1)
     for head, out_buf in enumerate((oa, ob)):
         others = out_buf.at[pl.ds(0, (group - 1) * tok)]
         pltpu.make_async_copy(others, others, osend_sem.at[head]).wait()
@@ -292,15 +311,15 @@
     slab = group * tok
     tiles, slots = tile_list.shape
     smem = pl.BlockSpec(memory_space=pltpu.SMEM)
-    anywhere = pl.BlockSpec(memory_space=pl.ANY)
+    hbm = pl.BlockSpec(memory_space=pltpu.HBM)
     narrow = pltpu.VMEM((slab, BLOCK, HD), jnp.bfloat16)
     wide = pltpu.VMEM((3 * slab, BLOCK, HD), jnp.bfloat16)
     dma = pltpu.SemaphoreType.DMA
     out = pl.pallas_call(
         functools.partial(kernel, n_tm, n_tm // 2, group, tiles, slots),
-        out_shape=jax.ShapeDtypeStruct((tok, BLOCK, width), queries.dtype),
-        in_specs=[smem, smem, anywhere, anywhere, anywhere],
-        out_specs=anywhere,
+        out_shape=pltpu.VMEM((tok, BLOCK, width), queries.dtype),
+        in_specs=[smem, smem, hbm, hbm, hbm],
+        out_specs=pl.BlockSpec(memory_space=pltpu.VMEM),
         scratch_shapes=[
             narrow, wide, wide, narrow, wide, wide, narrow, narrow,
             pltpu.VMEM((TILE, slots * TILE), jnp.float32),

time: 85.5 us -> 83.7 us (0.979)
  the two profiles are of different devices: /device:TPU:27 before, /device:TPU:7 now
where the time goes in v3:
time: 83.7 us; the launch traced here: 83.5 us
  Pallas kernels  82.5 us (99%)
  local copies, waits for them, and re-layouts  1.02 us (1%)
    pallas_call x1, Pallas kernels, shards(): pl.pallas_call(functools.partial(kernel, n_tm, n_tm // 2, group, tiles, s...  82.5 us

profile of v3, /device:TPU:7, one launch (start us, length us, event | category | flops | bytes accessed | tf_op | source)
XLA Modules:
  0.0 83.5 jit_solution(3115697598601401877)
XLA Ops:
  0.0 82.5 %shard_map.55 = bf16[3,48,4096]{2,1,0:T(8,128)(2,1)S(1)} custom-call(s32[6,7]{1,0:T(8,128)} %list_ref.1, s32[6]{0:T(128)} %count_ref.1, bf16[3,48,4096]{2,1,0:T(8,128)(2,1)} %bitcast.5, bf16[3,48,4096]{2,1,0:T(8,128)(2,1)} %bitcast.6, bf16[3,48,4096]{2,1,0:T(8,128)(2,1)} %bitcast.7), custom_call_target="tpu_custom_call" | custom-call | tf_op jit(solution)/shard_map/pallas_call | solution.py:318
  82.5 1.0 %copy.7 = bf16[144,4096]{1,0:T(8,128)(2,1)} copy(bf16[144,4096]{1,0:T(8,128)(2,1)S(1)} %bitcast.4) | data formatting | bytes 2359296
